TPU v7x, 32 devices: a whole 2x2x4 slice. The times are simulated.
32 devices in a mesh: grp: 2 (over x), obs: 16 (over z, y, core).
Axes of the slice: x: 2, y: 2, z: 4, core: 2. Of those that a mesh axis runs over, the one named last changes fastest.
Arguments:
- anomalies: bfloat16 [512, 16384], P(('grp', 'obs')), parts along dimension 0, may hold values from -6 to 6
- innovations: bfloat16 [512, 16384], P(('grp', 'obs')), parts along dimension 0, may hold values from -6 to 6
- sort_order: int32 [32768], P(('grp', 'obs')), parts along dimension 0, may hold values from 0 to 16383, as said below
- obs_error: float32 [32768], P(('grp', 'obs')), parts along dimension 0, may hold values from 0.2 to 2
Outputs:
- gain_product: float32 [32768, 256], P(('grp', 'obs')), parts along dimension 0
There are 2 independent parts, one for each index of `grp`. A program takes and returns all parts, laid end to end along the dimension named above; each array names one. Nothing has to cross between parts.
Inputs may be any that keep to these rules, and one draw needn't show every extreme that they name: Each acquisition index appears exactly once, and sort_order[p] lies in the same aligned block of 128 positions as p.
All inputs are finite; a program needn't handle non-finite values.
Results may differ from a plain program's by a relative error of at most 0.0025.
Values may be sent and summed in bfloat16 or wider, within the bound.
A program may use at most 64 MiB of HBM per device.

v0:
```python
import jax
import jax.numpy as jnp
from jax import lax
from jax.sharding import PartitionSpec as P


def shifted(shard, axis, by):
    peers = lax.axis_size(axis)
    pairs = [(i, i + by) for i in range(peers) if 0 <= i + by < peers]
    return lax.ppermute(shard, axis, pairs)


def gaspari(z):
    inner = z * z * (z * (z * (-0.25 * z + 0.5) + 0.625) - 5.0 / 3.0) + 1.0
    zs = jnp.maximum(z, 1.0)
    outer = (
        zs * zs * (zs * (zs * (zs / 12.0 - 0.5) + 0.625) + 5.0 / 3.0)
        - 5.0 * zs
        + 4.0
        - 2.0 / (3.0 * zs)
    )
    return jnp.where(z <= 1.0, inner, jnp.where(z < 2.0, outer, 0.0 * z))


def taper_scale(first_row, rows, cols, offset, half_width, members):
    row_ids = first_row + lax.iota(jnp.int32, rows)
    col_ids = lax.iota(jnp.int32, cols) + offset * cols
    dist = jnp.abs(row_ids[:, None] - col_ids[None, :]).astype(jnp.float32)
    return gaspari(dist / half_width) / (members - 1.0)


def permute_blocks(values, selector, width, blocks):
    shaped = values.reshape(values.shape[0], blocks, width)
    moved = jnp.einsum("mbi,bij->mbj", shaped, selector, preferred_element_type=jnp.float32)
    return moved.astype(jnp.bfloat16).reshape(values.shape[0], blocks * width)


def on_device(anomalies, innovations, sort_order, obs_error):
    raw_y, raw_d = (
        lax.all_to_all(anomalies, "obs", split_axis=1, concat_axis=0, tiled=True),
        lax.all_to_all(innovations, "obs", split_axis=1, concat_axis=0, tiled=True),
    )
    members = raw_y.shape[0]
    panel = raw_y.shape[1]
    width = min(128, panel)
    blocks = panel // width
    local_ids = (sort_order % width).reshape(blocks, width)
    selector = (lax.iota(jnp.int32, width)[None, :, None] == local_ids[:, None, :]).astype(
        jnp.bfloat16
    )
    y_here = permute_blocks(raw_y, selector, width, blocks)
    d_here = permute_blocks(raw_d, selector, width, blocks)
    block = min(512, panel)
    half_width = panel // 2 * 1.0

    def tile_rows(first, y_cols, offset):
        row_part = lax.slice_in_dim(y_here, first, first + block, axis=1)
        gram = lax.dot_general(
            row_part, y_cols, (((0,), (0,)), ((), ())), preferred_element_type=jnp.float32
        )
        return (gram * taper_scale(first, block, panel, offset, half_width, members * 1.0)).astype(
            jnp.bfloat16
        )

    def apply_rows(weights, d_cols):
        return lax.dot_general(
            weights, d_cols, (((1,), (1,)), ((), ())), preferred_element_type=jnp.float32
        )

    pieces = []
    low_y, low_d = shifted((y_here, d_here), "obs", 1)
    up_y, up_d = shifted((y_here, d_here), "obs", -1)
    for first in range(0, panel, block):
        acc = apply_rows(tile_rows(first, y_here, 0), d_here)
        acc = acc + apply_rows(tile_rows(first, low_y, -1), low_d)
        acc = acc + apply_rows(tile_rows(first, up_y, 1), up_d)
        pieces.append(acc)
    total = jnp.concatenate(pieces, axis=0)
    return total + obs_error[:, None] * d_here.T.astype(jnp.float32)


def solution(mesh):
    return jax.shard_map(
        on_device,
        mesh=mesh,
        in_specs=(
            P(("grp", "obs"), None),
            P(("grp", "obs"), None),
            P(("grp", "obs")),
            P(("grp", "obs")),
        ),
        out_specs=P(("grp", "obs"), None),
        check_vma=False,
    )
```

profile of v0, /device:TPU:1, one launch (start us, length us, event | category | flops | bytes accessed | tf_op | source)
XLA Modules:
  0.0 76.1 jit_solution(12527095984979136979)
XLA Ops:
  0.0 0.0 copy-start
  0.0 1.9 %copy.19 = bf16[2,16,8,1024]{3,2,0,1:T(8,128)(2,1)} copy(bf16[2,16,8,1024]{3,2,1,0:T(8,128)(2,1)} %bitcast.47) | data formatting | bytes 1048576 | tf_op jit(solution)/shard_map/all_to_all | solution.py:41
  1.9 7.3 %all-to-all-start.1 = ((bf16[16,16,1024]{2,0,1:T(8,128)(2,1)}), bf16[16,16,1024]{2,0,1:T(8,128)(2,1)S(1)}, u32[]{:S(2)}, u32[]{:S(2)}) async-start(bf16[16,16,1024]{2,0,1:T(8,128)(2,1)} %bitcast.37), calls=%async_computation.1 | async-start | bytes 1048576 | tf_op jit(solution)/shard_map/all_to_all | solution.py:41
  9.3 0.0 copy-done
  9.3 0.0 copy-start.2
  9.3 0.8 %copy.20 = bf16[2,16,8,1024]{3,2,0,1:T(8,128)(2,1)} copy(bf16[2,16,8,1024]{3,2,1,0:T(8,128)(2,1)S(1)} %bitcast.48) | data formatting | bytes 1048576 | tf_op jit(solution)/shard_map/all_to_all | solution.py:40
  10.1 13.2 %all-to-all-done.1 = bf16[16,16,1024]{2,0,1:T(8,128)(2,1)S(1)} async-done(((bf16[16,16,1024]{2,0,1:T(8,128)(2,1)}), bf16[16,16,1024]{2,0,1:T(8,128)(2,1)S(1)}, u32[]{:S(2)}, u32[]{:S(2)}) %all-to-all-start.1) | async-done | bytes 524320 | tf_op jit(solution)/shard_map/all_to_all | solution.py:41
  23.4 4.5 %all-to-all-start = ((bf16[16,16,1024]{2,0,1:T(8,128)(2,1)}), bf16[16,16,1024]{2,0,1:T(8,128)(2,1)S(1)}, u32[]{:S(2)}, u32[]{:S(2)}) async-start(bf16[16,16,1024]{2,0,1:T(8,128)(2,1)} %bitcast.38), calls=%async_computation | async-start | bytes 1048576 | tf_op jit(solution)/shard_map/all_to_all | solution.py:40
  27.9 0.0 copy-done.2
  27.9 0.1 copy.12
  28.0 0.3 convolution_convert_fusion
  28.4 3.5 %collective-permute-start.1 = (bf16[256,1024]{0,1:T(8,128)(2,1)S(1)}, bf16[256,1024]{0,1:T(8,128)(2,1)S(1)}, u32[]{:S(2)}, u32[]{:S(2)}) collective-permute-start(bf16[256,1024]{0,1:T(8,128)(2,1)S(1)} %bitcast.39), channel_id=1, source_target_pairs={{0,1},{1,2},{2,3},{3,4},{4,5},{5,6},{6,7},{7,8},{8,9},{9,10},{10,1... | collective-permute-start | bytes 1572872 | tf_op jit(solution)/shard_map/ppermute | solution.py:10
  31.9 1.9 %collective-permute-start.3 = (bf16[256,1024]{0,1:T(8,128)(2,1)S(1)}, bf16[256,1024]{0,1:T(8,128)(2,1)S(1)}, u32[]{:S(2)}, u32[]{:S(2)}) collective-permute-start(bf16[256,1024]{0,1:T(8,128)(2,1)S(1)} %bitcast.40), channel_id=1, source_target_pairs={{1,0},{2,1},{3,2},{4,3},{5,4},{6,5},{7,6},{8,7},{9,8},{10,9},{11,1... | collective-permute-start | bytes 1572872 | tf_op jit(solution)/shard_map/ppermute | solution.py:10
  33.8 8.1 %all-to-all-done = bf16[16,16,1024]{2,0,1:T(8,128)(2,1)S(1)} async-done(((bf16[16,16,1024]{2,0,1:T(8,128)(2,1)}), bf16[16,16,1024]{2,0,1:T(8,128)(2,1)S(1)}, u32[]{:S(2)}, u32[]{:S(2)}) %all-to-all-start) | async-done | bytes 524320 | tf_op jit(solution)/shard_map/all_to_all | solution.py:40
  41.9 0.1 copy.11
  42.0 0.3 convolution_convert_fusion.1
  42.4 2.5 %collective-permute-start = (bf16[256,1024]{0,1:T(8,128)(2,1)S(1)}, bf16[256,1024]{0,1:T(8,128)(2,1)S(1)}, u32[]{:S(2)}, u32[]{:S(2)}) collective-permute-start(bf16[256,1024]{0,1:T(8,128)(2,1)S(1)} %bitcast.49), channel_id=1, source_target_pairs={{0,1},{1,2},{2,3},{3,4},{4,5},{5,6},{6,7},{7,8},{8,9},{9,10},{10,1... | collective-permute-start | bytes 1572872 | tf_op jit(solution)/shard_map/ppermute | solution.py:10
  44.9 1.9 %collective-permute-start.2 = (bf16[256,1024]{0,1:T(8,128)(2,1)S(1)}, bf16[256,1024]{0,1:T(8,128)(2,1)}, u32[]{:S(2)}, u32[]{:S(2)}) collective-permute-start(bf16[256,1024]{0,1:T(8,128)(2,1)S(1)} %bitcast.50), channel_id=1, source_target_pairs={{1,0},{2,1},{3,2},{4,3},{5,4},{6,5},{7,6},{8,7},{9,8},{10,9},{11,1... | collective-permute-start | bytes 1572872 | tf_op jit(solution)/shard_map/ppermute | solution.py:10
  46.8 3.8 %fusion.7 = f32[512,256]{1,0:T(8,128)} fusion(bf16[256,1024]{0,1:T(8,128)(2,1)S(1)} %bitcast.41, bf16[256,1024]{0,1:T(8,128)(2,1)S(1)} %bitcast.51, s32[512]{0:T(512)S(1)} %iota_add_fusion.2), kind=kOutput, calls=%fused_computation.43 | convolution fusion | flops 555745280 | bytes 1837056 | tf_op jit(solution)/shard_map/dot_general | solution.py:66
  50.6 2.8 %fusion.6 = f32[512,256]{1,0:T(8,128)S(1)} fusion(bf16[256,1024]{0,1:T(8,128)(2,1)S(1)} %bitcast.42, bf16[256,1024]{0,1:T(8,128)(2,1)S(1)} %bitcast.52), kind=kOutput, calls=%fused_computation.42 | convolution fusion | flops 555745280 | bytes 1835008 | tf_op jit(solution)/shard_map/dot_general | solution.py:66
  53.3 0.0 collective-permute-done.1
  53.3 4.8 %collective-permute-done = bf16[256,1024]{0,1:T(8,128)(2,1)S(1)} collective-permute-done((bf16[256,1024]{0,1:T(8,128)(2,1)S(1)}, bf16[256,1024]{0,1:T(8,128)(2,1)S(1)}, u32[]{:S(2)}, u32[]{:S(2)}) %collective-permute-start) | collective-permute-done | bytes 524320 | tf_op jit(solution)/shard_map/ppermute | solution.py:10
  58.1 4.8 %convolution_add_fusion.1 = f32[512,256]{1,0:T(8,128)} fusion(f32[512,256]{1,0:T(8,128)} %fusion.7, bf16[256,1024]{0,1:T(8,128)(2,1)S(1)} %collective-permute-done.1, bf16[256,1024]{0,1:T(8,128)(2,1)S(1)} %collective-permute-done, s32[512]{0:T(512)S(1)} %iota_add_fusion.2, s32[1024]{0:T(1024)S(1)} %iota_add_fusion.1, bf16[256,1024]{0,1:T(8,128)(2,1)S(1)} %bitcast.53), kind=kOutput, calls=%fused_computation.39 | convolution fusion | flops 555876352 | bytes 2365440 | tf_op jit(solution)/shard_map/dot_general | solution.py:66
  62.9 3.7 %convolution_add_fusion.3 = f32[512,256]{1,0:T(8,128)} fusion(f32[512,256]{1,0:T(8,128)S(1)} %fusion.6, bf16[256,1024]{0,1:T(8,128)(2,1)S(1)} %collective-permute-done.1, bf16[256,1024]{0,1:T(8,128)(2,1)S(1)} %collective-permute-done, s32[1024]{0:T(1024)S(1)} %iota_add_fusion.1, bf16[256,1024]{0,1:T(8,128)(2,1)S(1)} %bitcast.54), kind=kOutput, calls=%fused_computation.41 | convolution fusion | flops 555876352 | bytes 2363392 | tf_op jit(solution)/shard_map/dot_general | solution.py:66
  66.6 0.0 copy-start.3
  66.6 0.0 collective-permute-done.3
  66.6 0.0 collective-permute-done.2
  66.6 4.4 %convolution_add_fusion = f32[512,256]{1,0:T(8,128)S(1)} fusion(f32[512,256]{1,0:T(8,128)} %convolution_add_fusion.1, bf16[256,1024]{0,1:T(8,128)(2,1)S(1)} %collective-permute-done.3, bf16[256,1024]{0,1:T(8,128)(2,1)} %collective-permute-done.2, s32[512]{0:T(512)S(1)} %iota_add_fusion.2, s32[1024]{0:T(1024)S(1)} %iota_add_fusion, ...), kind=kOutput, calls=%fused_computation.38 | convolution fusion | flops 555876352 | bytes 2365440 | tf_op jit(solution)/shard_map/dot_general | solution.py:66
  71.0 0.0 copy-done.3
  71.0 4.0 %convolution_add_fusion.2 = f32[512,256]{1,0:T(8,128)S(1)} fusion(f32[512,256]{1,0:T(8,128)S(1)} %copy-done.3, bf16[256,1024]{0,1:T(8,128)(2,1)S(1)} %collective-permute-done.3, bf16[256,1024]{0,1:T(8,128)(2,1)} %collective-permute-done.2, s32[1024]{0:T(1024)S(1)} %iota_add_fusion, bf16[256,1024]{0,1:T(8,128)(2,1)S(1)} %bitcast.56), kind=kOutput, calls=%fused_computation.40 | convolution fusion | flops 555876352 | bytes 2363392 | tf_op jit(solution)/shard_map/dot_general | solution.py:66
  75.0 0.0 copy-done.1
  75.0 1.2 %maximum_add_fusion = f32[1024,256]{1,0:T(8,128)} fusion(f32[512,256]{1,0:T(8,128)S(1)} %convolution_add_fusion, f32[512,256]{1,0:T(8,128)S(1)} %convolution_add_fusion.2, f32[1024]{0:T(1024)S(1)} %copy-done.1, bf16[8,128,256]{2,1,0:T(8,128)(2,1)S(1)} %convolution_convert_fusion), kind=kLoop, calls=%fused_computation.44 | loop fusion | flops 1048576 | bytes 2625536 | tf_op jit(solution)/shard_map/add | solution.py:79
  (5 shorter events, 0.0 us)
Async XLA Ops:
  0.0 9.3 %copy-start = (bf16[16,16384]{1,0:T(8,128)(2,1)S(1)}, bf16[16,16384]{1,0:T(8,128)(2,1)}, u32[]{:S(2)}) copy-start(bf16[16,16384]{1,0:T(8,128)(2,1)} %param.4) | copy-start | bytes 1572868
  1.9 21.4 %all-to-all-start.1 = ((bf16[16,16,1024]{2,0,1:T(8,128)(2,1)}), bf16[16,16,1024]{2,0,1:T(8,128)(2,1)S(1)}, u32[]{:S(2)}, u32[]{:S(2)}) async-start(bf16[16,16,1024]{2,0,1:T(8,128)(2,1)} %bitcast.37), calls=%async_computation.1 | async-start | bytes 1048576 | tf_op jit(solution)/shard_map/all_to_all | solution.py:41
  9.3 18.6 %copy-start.2 = (s32[1024]{0:T(1024)S(1)}, s32[1024]{0:T(1024)}, u32[]{:S(2)}) copy-start(s32[1024]{0:T(1024)} %param.6) | copy-start | bytes 12292
  23.4 18.6 %all-to-all-start = ((bf16[16,16,1024]{2,0,1:T(8,128)(2,1)}), bf16[16,16,1024]{2,0,1:T(8,128)(2,1)S(1)}, u32[]{:S(2)}, u32[]{:S(2)}) async-start(bf16[16,16,1024]{2,0,1:T(8,128)(2,1)} %bitcast.38), calls=%async_computation | async-start | bytes 1048576 | tf_op jit(solution)/shard_map/all_to_all | solution.py:40
  28.4 25.0 %collective-permute-start.1 = (bf16[256,1024]{0,1:T(8,128)(2,1)S(1)}, bf16[256,1024]{0,1:T(8,128)(2,1)S(1)}, u32[]{:S(2)}, u32[]{:S(2)}) collective-permute-start(bf16[256,1024]{0,1:T(8,128)(2,1)S(1)} %bitcast.39), channel_id=1, source_target_pairs={{0,1},{1,2},{2,3},{3,4},{4,5},{5,6},{6,7},{7,8},{8,9},{9,10},{10,1... | collective-permute-start | bytes 1572872 | tf_op jit(solution)/shard_map/ppermute | solution.py:10
  31.9 34.7 %collective-permute-start.3 = (bf16[256,1024]{0,1:T(8,128)(2,1)S(1)}, bf16[256,1024]{0,1:T(8,128)(2,1)S(1)}, u32[]{:S(2)}, u32[]{:S(2)}) collective-permute-start(bf16[256,1024]{0,1:T(8,128)(2,1)S(1)} %bitcast.40), channel_id=1, source_target_pairs={{1,0},{2,1},{3,2},{4,3},{5,4},{6,5},{7,6},{8,7},{9,8},{10,9},{11,1... | collective-permute-start | bytes 1572872 | tf_op jit(solution)/shard_map/ppermute | solution.py:10
  42.4 15.7 %collective-permute-start = (bf16[256,1024]{0,1:T(8,128)(2,1)S(1)}, bf16[256,1024]{0,1:T(8,128)(2,1)S(1)}, u32[]{:S(2)}, u32[]{:S(2)}) collective-permute-start(bf16[256,1024]{0,1:T(8,128)(2,1)S(1)} %bitcast.49), channel_id=1, source_target_pairs={{0,1},{1,2},{2,3},{3,4},{4,5},{5,6},{6,7},{7,8},{8,9},{9,10},{10,1... | collective-permute-start | bytes 1572872 | tf_op jit(solution)/shard_map/ppermute | solution.py:10
  44.9 21.7 %collective-permute-start.2 = (bf16[256,1024]{0,1:T(8,128)(2,1)S(1)}, bf16[256,1024]{0,1:T(8,128)(2,1)}, u32[]{:S(2)}, u32[]{:S(2)}) collective-permute-start(bf16[256,1024]{0,1:T(8,128)(2,1)S(1)} %bitcast.50), channel_id=1, source_target_pairs={{1,0},{2,1},{3,2},{4,3},{5,4},{6,5},{7,6},{8,7},{9,8},{10,9},{11,1... | collective-permute-start | bytes 1572872 | tf_op jit(solution)/shard_map/ppermute | solution.py:10
  66.6 4.4 %copy-start.3 = (f32[512,256]{1,0:T(8,128)S(1)}, f32[512,256]{1,0:T(8,128)}, u32[]{:S(2)}) copy-start(f32[512,256]{1,0:T(8,128)} %convolution_add_fusion.3) | copy-start | bytes 1572868
  71.0 4.0 %copy-start.1 = (f32[1024]{0:T(1024)S(1)}, f32[1024]{0:T(1024)}, u32[]{:S(2)}) copy-start(f32[1024]{0:T(1024)} %param.7) | copy-start | bytes 12292
where the time goes:
time: 76.6 us; the launch traced here: 76.1 us
  waiting for transfers between devices  26.1 us (34%)
  matrix products  24 us (31%)
  starting transfers between devices  21.7 us (28%)
  local copies, waits for them, and re-layouts  2.97 us (4%)
  other arithmetic  1.21 us (2%)
    dot_general x6, matrix products, apply_rows(): lax.dot_general(weights, d_cols, (((1,), (1,)), ((), ())), preferred_elem...  23.3 us
    all_to_all x1, waiting for transfers between devices, on_device(): lax.all_to_all(innovations, 'obs', split_axis=1, concat_axis=0, tiled=True)  13.2 us
    ppermute x4, starting transfers between devices, shifted(): return lax.ppermute(shard, axis, pairs)  9.9 us
    all_to_all x1, waiting for transfers between devices, on_device(): lax.all_to_all(anomalies, 'obs', split_axis=1, concat_axis=0, tiled=True)  8.09 us
    all_to_all x1, starting transfers between devices, on_device(): lax.all_to_all(innovations, 'obs', split_axis=1, concat_axis=0, tiled=True)  7.35 us
    ppermute x4, waiting for transfers between devices, shifted(): return lax.ppermute(shard, axis, pairs)  4.78 us
    all_to_all x1, starting transfers between devices, on_device(): lax.all_to_all(anomalies, 'obs', split_axis=1, concat_axis=0, tiled=True)  4.5 us
    all_to_all x1, local copies, waits for them, and re-layouts, on_device(): lax.all_to_all(innovations, 'obs', split_axis=1, concat_axis=0, tiled=True)  1.93 us
  transfers between devices with their start and end apart: 6, of which 3 were waited for; matrix products, arithmetic and copies ran while one was open for 22% of the time, Pallas kernels for 0%

commit v1 on v0

--- a/solution.py
+++ b/solution.py
@@ -38,7 +38,12 @@
 def on_device(anomalies, innovations, sort_order, obs_error):
     raw_y, raw_d = (
         lax.all_to_all(anomalies, "obs", split_axis=1, concat_axis=0, tiled=True),
-        lax.all_to_all(innovations, "obs", split_axis=1, concat_axis=0, tiled=True),
+        jnp.concatenate(
+            lax.all_to_all(
+                jnp.stack(jnp.split(innovations, lax.axis_size("obs"), axis=1)), "obs", 0, 0
+            ),
+            axis=0,
+        ),
     )
     members = raw_y.shape[0]
     panel = raw_y.shape[1]

time: 76.6 us -> 97.8 us (1.28); the launches traced: 76.1 us -> 96.3 us
  local copies, waits for them, and re-layouts: 2.97 us -> 23.1 us
    unnamed x10 -> x25, local copies, waits for them, and re-layouts: 0.2 us -> 20.9 us
    all_to_all x1 -> x0, local copies, waits for them, and re-layouts: 1.93 us -> none  [on_device(): lax.all_to_all(innovations, 'obs', split_axis=1, concat_axis=0, tiled=True)]
    another operation x0 -> x1, local copies, waits for them, and re-layouts: none -> 1.37 us  [on_device(): jnp.stack(jnp.split(innovations, lax.axis_size('obs'), axis=1))]
  transfers between devices with their start and end apart: 6 -> 6, of which waited for: 3 -> 3; matrix products, arithmetic and copies ran while one was open for 22% -> 17% of each run, Pallas kernels for 0% -> 0%
where the time goes in v1:
time: 97.8 us; the launch traced here: 96.3 us
  waiting for transfers between devices  26.1 us (27%)
  matrix products  24 us (25%)
  local copies, waits for them, and re-layouts  23.1 us (24%)
  starting transfers between devices  21.7 us (22%)
  other arithmetic  1.21 us (1%)
    dot_general x6, matrix products, apply_rows(): lax.dot_general(weights, d_cols, (((1,), (1,)), ((), ())), preferred_elem...  23.3 us
    unnamed x25, local copies, waits for them, and re-layouts  20.9 us
    all_to_all x1, waiting for transfers between devices, on_device(): lax.all_to_all(jnp.stack(jnp.split(innovations, lax.axis_size('obs'), axi...  13.2 us
    ppermute x4, starting transfers between devices, shifted(): return lax.ppermute(shard, axis, pairs)  9.89 us
    all_to_all x1, waiting for transfers between devices, on_device(): lax.all_to_all(anomalies, 'obs', split_axis=1, concat_axis=0, tiled=True)  8.1 us
    all_to_all x1, starting transfers between devices, on_device(): lax.all_to_all(jnp.stack(jnp.split(innovations, lax.axis_size('obs'), axi...  7.35 us
    ppermute x4, waiting for transfers between devices, shifted(): return lax.ppermute(shard, axis, pairs)  4.78 us
    all_to_all x1, starting transfers between devices, on_device(): lax.all_to_all(anomalies, 'obs', split_axis=1, concat_axis=0, tiled=True)  4.5 us
  transfers between devices with their start and end apart: 6, of which 3 were waited for; matrix products, arithmetic and copies ran while one was open for 17% of the time, Pallas kernels for 0%

profile of v1, /device:TPU:1, one launch (start us, length us, event | category | flops | bytes accessed | tf_op | source)
XLA Modules:
  0.0 96.3 jit_solution(12035970150470161992)
XLA Ops:
  0.0 1.4 %constant_dynamic-update-slice_fusion.15 = bf16[16,16,1024]{2,1,0:T(8,128)(2,1)} fusion(bf16[16,16384]{1,0:T(8,128)(2,1)} %param.5), kind=kLoop, calls=%fused_computation.169 | loop fusion | bytes 65536
  1.4 1.4 %constant_dynamic-update-slice_fusion.14 = bf16[16,16,1024]{2,1,0:T(8,128)(2,1)} fusion(bf16[16,16,1024]{2,1,0:T(8,128)(2,1)} %constant_dynamic-update-slice_fusion.15, bf16[16,16384]{1,0:T(8,128)(2,1)} %param.5), kind=kLoop, calls=%fused_computation.168 | loop fusion | bytes 65536
  2.8 1.4 %constant_dynamic-update-slice_fusion.13 = bf16[16,16,1024]{2,1,0:T(8,128)(2,1)} fusion(bf16[16,16,1024]{2,1,0:T(8,128)(2,1)} %constant_dynamic-update-slice_fusion.14, bf16[16,16384]{1,0:T(8,128)(2,1)} %param.5), kind=kLoop, calls=%fused_computation.167 | loop fusion | bytes 65536
  4.2 1.4 %constant_dynamic-update-slice_fusion.12 = bf16[16,16,1024]{2,1,0:T(8,128)(2,1)} fusion(bf16[16,16,1024]{2,1,0:T(8,128)(2,1)} %constant_dynamic-update-slice_fusion.13, bf16[16,16384]{1,0:T(8,128)(2,1)} %param.5), kind=kLoop, calls=%fused_computation.166 | loop fusion | bytes 65536
  5.6 1.4 %constant_dynamic-update-slice_fusion.11 = bf16[16,16,1024]{2,1,0:T(8,128)(2,1)} fusion(bf16[16,16,1024]{2,1,0:T(8,128)(2,1)} %constant_dynamic-update-slice_fusion.12, bf16[16,16384]{1,0:T(8,128)(2,1)} %param.5), kind=kLoop, calls=%fused_computation.165 | loop fusion | bytes 65536
  6.9 1.4 %constant_dynamic-update-slice_fusion.10 = bf16[16,16,1024]{2,1,0:T(8,128)(2,1)} fusion(bf16[16,16,1024]{2,1,0:T(8,128)(2,1)} %constant_dynamic-update-slice_fusion.11, bf16[16,16384]{1,0:T(8,128)(2,1)} %param.5), kind=kLoop, calls=%fused_computation.164 | loop fusion | bytes 65536
  8.3 1.4 %constant_dynamic-update-slice_fusion.9 = bf16[16,16,1024]{2,1,0:T(8,128)(2,1)} fusion(bf16[16,16,1024]{2,1,0:T(8,128)(2,1)} %constant_dynamic-update-slice_fusion.10, bf16[16,16384]{1,0:T(8,128)(2,1)} %param.5), kind=kLoop, calls=%fused_computation.163 | loop fusion | bytes 65536
  9.7 1.4 %constant_dynamic-update-slice_fusion.8 = bf16[16,16,1024]{2,1,0:T(8,128)(2,1)} fusion(bf16[16,16,1024]{2,1,0:T(8,128)(2,1)} %constant_dynamic-update-slice_fusion.9, bf16[16,16384]{1,0:T(8,128)(2,1)} %param.5), kind=kLoop, calls=%fused_computation.162 | loop fusion | bytes 65536
  11.1 1.4 %constant_dynamic-update-slice_fusion.7 = bf16[16,16,1024]{2,1,0:T(8,128)(2,1)} fusion(bf16[16,16,1024]{2,1,0:T(8,128)(2,1)} %constant_dynamic-update-slice_fusion.8, bf16[16,16384]{1,0:T(8,128)(2,1)} %param.5), kind=kLoop, calls=%fused_computation.161 | loop fusion | bytes 65536
  12.4 1.4 %constant_dynamic-update-slice_fusion.6 = bf16[16,16,1024]{2,1,0:T(8,128)(2,1)} fusion(bf16[16,16,1024]{2,1,0:T(8,128)(2,1)} %constant_dynamic-update-slice_fusion.7, bf16[16,16384]{1,0:T(8,128)(2,1)} %param.5), kind=kLoop, calls=%fused_computation.160 | loop fusion | bytes 65536
  13.8 1.4 %constant_dynamic-update-slice_fusion.5 = bf16[16,16,1024]{2,1,0:T(8,128)(2,1)} fusion(bf16[16,16,1024]{2,1,0:T(8,128)(2,1)} %constant_dynamic-update-slice_fusion.6, bf16[16,16384]{1,0:T(8,128)(2,1)} %param.5), kind=kLoop, calls=%fused_computation.159 | loop fusion | bytes 65536
  15.2 1.4 %constant_dynamic-update-slice_fusion.4 = bf16[16,16,1024]{2,1,0:T(8,128)(2,1)} fusion(bf16[16,16,1024]{2,1,0:T(8,128)(2,1)} %constant_dynamic-update-slice_fusion.5, bf16[16,16384]{1,0:T(8,128)(2,1)} %param.5), kind=kLoop, calls=%fused_computation.158 | loop fusion | bytes 65536
  16.6 1.4 %constant_dynamic-update-slice_fusion.3 = bf16[16,16,1024]{2,1,0:T(8,128)(2,1)} fusion(bf16[16,16,1024]{2,1,0:T(8,128)(2,1)} %constant_dynamic-update-slice_fusion.4, bf16[16,16384]{1,0:T(8,128)(2,1)} %param.5), kind=kLoop, calls=%fused_computation.157 | loop fusion | bytes 65536
  17.9 1.4 %constant_dynamic-update-slice_fusion.2 = bf16[16,16,1024]{2,1,0:T(8,128)(2,1)} fusion(bf16[16,16,1024]{2,1,0:T(8,128)(2,1)} %constant_dynamic-update-slice_fusion.3, bf16[16,16384]{1,0:T(8,128)(2,1)} %param.5), kind=kLoop, calls=%fused_computation.156 | loop fusion | bytes 65536
  19.3 1.4 %constant_dynamic-update-slice_fusion.1 = bf16[16,16,1024]{2,1,0:T(8,128)(2,1)} fusion(bf16[16,16,1024]{2,1,0:T(8,128)(2,1)} %constant_dynamic-update-slice_fusion.2, bf16[16,16384]{1,0:T(8,128)(2,1)} %param.5), kind=kLoop, calls=%fused_computation.155 | loop fusion | bytes 65536
  20.7 1.4 %constant_dynamic-update-slice_fusion = bf16[16,16,1024]{2,1,0:T(8,128)(2,1)} fusion(bf16[16,16,1024]{2,1,0:T(8,128)(2,1)} %constant_dynamic-update-slice_fusion.1, bf16[16,16384]{1,0:T(8,128)(2,1)} %param.5), kind=kLoop, calls=%fused_computation.154 | loop fusion | bytes 65536 | tf_op jit(solution)/shard_map/stack | solution.py:43
  22.0 7.3 %all-to-all-start.1 = ((bf16[16,16,1024]{2,1,0:T(8,128)(2,1)}), bf16[16,16,1024]{2,1,0:T(8,128)(2,1)S(1)}, u32[]{:S(2)}, u32[]{:S(2)}) async-start(bf16[16,16,1024]{2,1,0:T(8,128)(2,1)} %constant_dynamic-update-slice_fusion), calls=%async_computation.1 | async-start | bytes 1048576 | tf_op jit(solution)/shard_map/all_to_all | solution.py:42
  30.2 13.2 %all-to-all-done.1 = bf16[16,16,1024]{2,1,0:T(8,128)(2,1)S(1)} async-done(((bf16[16,16,1024]{2,1,0:T(8,128)(2,1)}), bf16[16,16,1024]{2,1,0:T(8,128)(2,1)S(1)}, u32[]{:S(2)}, u32[]{:S(2)}) %all-to-all-start.1) | async-done | bytes 524320 | tf_op jit(solution)/shard_map/all_to_all | solution.py:42
  43.5 4.5 %all-to-all-start = ((bf16[16,16,1024]{2,0,1:T(8,128)(2,1)}), bf16[16,16,1024]{2,0,1:T(8,128)(2,1)S(1)}, u32[]{:S(2)}, u32[]{:S(2)}) async-start(bf16[16,16,1024]{2,0,1:T(8,128)(2,1)} %bitcast.65), calls=%async_computation | async-start | bytes 1048576 | tf_op jit(solution)/shard_map/all_to_all | solution.py:40
  48.5 3.5 %collective-permute-start.1 = (bf16[256,1024]{0,1:T(8,128)(2,1)S(1)}, bf16[256,1024]{0,1:T(8,128)(2,1)S(1)}, u32[]{:S(2)}, u32[]{:S(2)}) collective-permute-start(bf16[256,1024]{0,1:T(8,128)(2,1)S(1)} %bitcast.66), channel_id=1, source_target_pairs={{0,1},{1,2},{2,3},{3,4},{4,5},{5,6},{6,7},{7,8},{8,9},{9,10},{10,1... | collective-permute-start | bytes 1572872 | tf_op jit(solution)/shard_map/ppermute | solution.py:10
  52.0 1.9 %collective-permute-start.3 = (bf16[256,1024]{0,1:T(8,128)(2,1)S(1)}, bf16[256,1024]{0,1:T(8,128)(2,1)S(1)}, u32[]{:S(2)}, u32[]{:S(2)}) collective-permute-start(bf16[256,1024]{0,1:T(8,128)(2,1)S(1)} %bitcast.67), channel_id=1, source_target_pairs={{1,0},{2,1},{3,2},{4,3},{5,4},{6,5},{7,6},{8,7},{9,8},{10,9},{11,1... | collective-permute-start | bytes 1572872 | tf_op jit(solution)/shard_map/ppermute | solution.py:10
  54.0 8.1 %all-to-all-done = bf16[16,16,1024]{2,0,1:T(8,128)(2,1)S(1)} async-done(((bf16[16,16,1024]{2,0,1:T(8,128)(2,1)}), bf16[16,16,1024]{2,0,1:T(8,128)(2,1)S(1)}, u32[]{:S(2)}, u32[]{:S(2)}) %all-to-all-start) | async-done | bytes 524320 | tf_op jit(solution)/shard_map/all_to_all | solution.py:40
  62.5 2.5 %collective-permute-start = (bf16[256,1024]{0,1:T(8,128)(2,1)S(1)}, bf16[256,1024]{0,1:T(8,128)(2,1)S(1)}, u32[]{:S(2)}, u32[]{:S(2)}) collective-permute-start(bf16[256,1024]{0,1:T(8,128)(2,1)S(1)} %bitcast.75), channel_id=1, source_target_pairs={{0,1},{1,2},{2,3},{3,4},{4,5},{5,6},{6,7},{7,8},{8,9},{9,10},{10,1... | collective-permute-start | bytes 1572872 | tf_op jit(solution)/shard_map/ppermute | solution.py:10
  65.0 1.9 %collective-permute-start.2 = (bf16[256,1024]{0,1:T(8,128)(2,1)S(1)}, bf16[256,1024]{0,1:T(8,128)(2,1)}, u32[]{:S(2)}, u32[]{:S(2)}) collective-permute-start(bf16[256,1024]{0,1:T(8,128)(2,1)S(1)} %bitcast.76), channel_id=1, source_target_pairs={{1,0},{2,1},{3,2},{4,3},{5,4},{6,5},{7,6},{8,7},{9,8},{10,9},{11,1... | collective-permute-start | bytes 1572872 | tf_op jit(solution)/shard_map/ppermute | solution.py:10
  66.9 3.8 %fusion.7 = f32[512,256]{1,0:T(8,128)} fusion(bf16[256,1024]{0,1:T(8,128)(2,1)S(1)} %bitcast.68, bf16[256,1024]{0,1:T(8,128)(2,1)S(1)} %bitcast.77, s32[512]{0:T(512)S(1)} %iota_add_fusion.2), kind=kOutput, calls=%fused_computation.43 | convolution fusion | flops 555745280 | bytes 1837056 | tf_op jit(solution)/shard_map/dot_general | solution.py:71
  70.7 2.8 %fusion.6 = f32[512,256]{1,0:T(8,128)S(1)} fusion(bf16[256,1024]{0,1:T(8,128)(2,1)S(1)} %bitcast.69, bf16[256,1024]{0,1:T(8,128)(2,1)S(1)} %bitcast.78), kind=kOutput, calls=%fused_computation.42 | convolution fusion | flops 555745280 | bytes 1835008 | tf_op jit(solution)/shard_map/dot_general | solution.py:71
  73.5 4.8 %collective-permute-done = bf16[256,1024]{0,1:T(8,128)(2,1)S(1)} collective-permute-done((bf16[256,1024]{0,1:T(8,128)(2,1)S(1)}, bf16[256,1024]{0,1:T(8,128)(2,1)S(1)}, u32[]{:S(2)}, u32[]{:S(2)}) %collective-permute-start) | collective-permute-done | bytes 524320 | tf_op jit(solution)/shard_map/ppermute | solution.py:10
  78.2 4.8 %convolution_add_fusion.1 = f32[512,256]{1,0:T(8,128)} fusion(f32[512,256]{1,0:T(8,128)} %fusion.7, bf16[256,1024]{0,1:T(8,128)(2,1)S(1)} %collective-permute-done.1, bf16[256,1024]{0,1:T(8,128)(2,1)S(1)} %collective-permute-done, s32[512]{0:T(512)S(1)} %iota_add_fusion.2, s32[1024]{0:T(1024)S(1)} %iota_add_fusion.1, bf16[256,1024]{0,1:T(8,128)(2,1)S(1)} %bitcast.79), kind=kOutput, calls=%fused_computation.39 | convolution fusion | flops 555876352 | bytes 2365440 | tf_op jit(solution)/shard_map/dot_general | solution.py:71
  83.0 3.7 %convolution_add_fusion.3 = f32[512,256]{1,0:T(8,128)} fusion(f32[512,256]{1,0:T(8,128)S(1)} %fusion.6, bf16[256,1024]{0,1:T(8,128)(2,1)S(1)} %collective-permute-done.1, bf16[256,1024]{0,1:T(8,128)(2,1)S(1)} %collective-permute-done, s32[1024]{0:T(1024)S(1)} %iota_add_fusion.1, bf16[256,1024]{0,1:T(8,128)(2,1)S(1)} %bitcast.80), kind=kOutput, calls=%fused_computation.41 | convolution fusion | flops 555876352 | bytes 2363392 | tf_op jit(solution)/shard_map/dot_general | solution.py:71
  86.7 4.4 %convolution_add_fusion = f32[512,256]{1,0:T(8,128)S(1)} fusion(f32[512,256]{1,0:T(8,128)} %convolution_add_fusion.1, bf16[256,1024]{0,1:T(8,128)(2,1)S(1)} %collective-permute-done.3, bf16[256,1024]{0,1:T(8,128)(2,1)} %collective-permute-done.2, s32[512]{0:T(512)S(1)} %iota_add_fusion.2, s32[1024]{0:T(1024)S(1)} %iota_add_fusion, ...), kind=kOutput, calls=%fused_computation.38 | convolution fusion | flops 555876352 | bytes 2365440 | tf_op jit(solution)/shard_map/dot_general | solution.py:71
  91.1 4.0 %convolution_add_fusion.2 = f32[512,256]{1,0:T(8,128)S(1)} fusion(f32[512,256]{1,0:T(8,128)S(1)} %copy-done.3, bf16[256,1024]{0,1:T(8,128)(2,1)S(1)} %collective-permute-done.3, bf16[256,1024]{0,1:T(8,128)(2,1)} %collective-permute-done.2, s32[1024]{0:T(1024)S(1)} %iota_add_fusion, bf16[256,1024]{0,1:T(8,128)(2,1)S(1)} %bitcast.82), kind=kOutput, calls=%fused_computation.40 | convolution fusion | flops 555876352 | bytes 2363392 | tf_op jit(solution)/shard_map/dot_general | solution.py:71
  95.1 1.2 %maximum_add_fusion = f32[1024,256]{1,0:T(8,128)} fusion(f32[512,256]{1,0:T(8,128)S(1)} %convolution_add_fusion, f32[512,256]{1,0:T(8,128)S(1)} %convolution_add_fusion.2, f32[1024]{0:T(1024)S(1)} %copy-done.1, bf16[8,128,256]{2,1,0:T(8,128)(2,1)S(1)} %convolution_convert_fusion), kind=kLoop, calls=%fused_computation.44 | loop fusion | flops 1048576 | bytes 2625536 | tf_op jit(solution)/shard_map/add | solution.py:84
  (20 shorter events, 1.7 us)
Async XLA Ops:
  0.0 29.4 %copy-start = (bf16[16,16384]{1,0:T(8,128)(2,1)S(1)}, bf16[16,16384]{1,0:T(8,128)(2,1)}, u32[]{:S(2)}) copy-start(bf16[16,16384]{1,0:T(8,128)(2,1)} %param.4) | copy-start | bytes 1572868
  22.0 21.4 %all-to-all-start.1 = ((bf16[16,16,1024]{2,1,0:T(8,128)(2,1)}), bf16[16,16,1024]{2,1,0:T(8,128)(2,1)S(1)}, u32[]{:S(2)}, u32[]{:S(2)}) async-start(bf16[16,16,1024]{2,1,0:T(8,128)(2,1)} %constant_dynamic-update-slice_fusion), calls=%async_computation.1 | async-start | bytes 1048576 | tf_op jit(solution)/shard_map/all_to_all | solution.py:42
  29.4 18.6 %copy-start.2 = (s32[1024]{0:T(1024)S(1)}, s32[1024]{0:T(1024)}, u32[]{:S(2)}) copy-start(s32[1024]{0:T(1024)} %param.6) | copy-start | bytes 12292
  43.5 18.6 %all-to-all-start = ((bf16[16,16,1024]{2,0,1:T(8,128)(2,1)}), bf16[16,16,1024]{2,0,1:T(8,128)(2,1)S(1)}, u32[]{:S(2)}, u32[]{:S(2)}) async-start(bf16[16,16,1024]{2,0,1:T(8,128)(2,1)} %bitcast.65), calls=%async_computation | async-start | bytes 1048576 | tf_op jit(solution)/shard_map/all_to_all | solution.py:40
  48.5 25.0 %collective-permute-start.1 = (bf16[256,1024]{0,1:T(8,128)(2,1)S(1)}, bf16[256,1024]{0,1:T(8,128)(2,1)S(1)}, u32[]{:S(2)}, u32[]{:S(2)}) collective-permute-start(bf16[256,1024]{0,1:T(8,128)(2,1)S(1)} %bitcast.66), channel_id=1, source_target_pairs={{0,1},{1,2},{2,3},{3,4},{4,5},{5,6},{6,7},{7,8},{8,9},{9,10},{10,1... | collective-permute-start | bytes 1572872 | tf_op jit(solution)/shard_map/ppermute | solution.py:10
  52.0 34.7 %collective-permute-start.3 = (bf16[256,1024]{0,1:T(8,128)(2,1)S(1)}, bf16[256,1024]{0,1:T(8,128)(2,1)S(1)}, u32[]{:S(2)}, u32[]{:S(2)}) collective-permute-start(bf16[256,1024]{0,1:T(8,128)(2,1)S(1)} %bitcast.67), channel_id=1, source_target_pairs={{1,0},{2,1},{3,2},{4,3},{5,4},{6,5},{7,6},{8,7},{9,8},{10,9},{11,1... | collective-permute-start | bytes 1572872 | tf_op jit(solution)/shard_map/ppermute | solution.py:10
  62.5 15.7 %collective-permute-start = (bf16[256,1024]{0,1:T(8,128)(2,1)S(1)}, bf16[256,1024]{0,1:T(8,128)(2,1)S(1)}, u32[]{:S(2)}, u32[]{:S(2)}) collective-permute-start(bf16[256,1024]{0,1:T(8,128)(2,1)S(1)} %bitcast.75), channel_id=1, source_target_pairs={{0,1},{1,2},{2,3},{3,4},{4,5},{5,6},{6,7},{7,8},{8,9},{9,10},{10,1... | collective-permute-start | bytes 1572872 | tf_op jit(solution)/shard_map/ppermute | solution.py:10
  65.0 21.7 %collective-permute-start.2 = (bf16[256,1024]{0,1:T(8,128)(2,1)S(1)}, bf16[256,1024]{0,1:T(8,128)(2,1)}, u32[]{:S(2)}, u32[]{:S(2)}) collective-permute-start(bf16[256,1024]{0,1:T(8,128)(2,1)S(1)} %bitcast.76), channel_id=1, source_target_pairs={{1,0},{2,1},{3,2},{4,3},{5,4},{6,5},{7,6},{8,7},{9,8},{10,9},{11,1... | collective-permute-start | bytes 1572872 | tf_op jit(solution)/shard_map/ppermute | solution.py:10
  86.7 4.4 %copy-start.3 = (f32[512,256]{1,0:T(8,128)S(1)}, f32[512,256]{1,0:T(8,128)}, u32[]{:S(2)}) copy-start(f32[512,256]{1,0:T(8,128)} %convolution_add_fusion.3) | copy-start | bytes 1572868
  91.1 4.0 %copy-start.1 = (f32[1024]{0:T(1024)S(1)}, f32[1024]{0:T(1024)}, u32[]{:S(2)}) copy-start(f32[1024]{0:T(1024)} %param.7) | copy-start | bytes 12292
